TPU v7x, 32 devices: a whole 2x2x4 slice. The times are simulated.
32 devices in a mesh: ctx: 8 (over y, x, core), fsdp: 4 (over z).
Axes of the slice: x: 2, y: 2, z: 4, core: 2. Of those that a mesh axis runs over, the one named last changes fastest.
Arguments:
- layer_input: bfloat16 [4, 1024, 1024], P('fsdp', 'ctx'), may hold values from -6 to 6
- token_positions: int32 [4, 1024], P('fsdp'), may hold values from 0 to 1023, as said below
- attention_gain: float32 [1024], replicated, may hold values from 0.5 to 1.5
- query_weight: bfloat16 [1024, 2048], P('fsdp'), may hold values from -0.1875 to 0.1875
- key_matrix: bfloat16 [1024, 1024], P('fsdp'), may hold values from -0.1875 to 0.1875
- value_matrix: bfloat16 [1024, 1024], P('fsdp'), may hold values from -0.1875 to 0.1875
- query_gain: float32 [128], replicated, may hold values from 0.5 to 1.5
- key_norm_gain: float32 [128], replicated, may hold values from 0.5 to 1.5
- output_weight: bfloat16 [2048, 1024], P('fsdp'), may hold values from -1 to 1
- feedforward_gain: float32 [1024], replicated, may hold values from 0.5 to 1.5
- gate_weight: bfloat16 [1024, 3072], P('fsdp'), may hold values from -0.1875 to 0.1875
- up_weight: bfloat16 [1024, 3072], P('fsdp'), may hold values from -0.1875 to 0.1875
- down_weight: bfloat16 [3072, 1024], P('fsdp'), may hold values from -0.15625 to 0.15625
- out_cotangent: bfloat16 [4, 1024, 1024], P('fsdp', 'ctx'), may hold values from -6 to 6
Outputs:
- layer_output: bfloat16 [4, 1024, 1024], P('fsdp', 'ctx')
- input_gradient: float32 [4, 1024, 1024], P('fsdp', 'ctx')
- attention_gain_gradient: float32 [1024], replicated
- query_gradient: float32 [1024, 2048], P(('ctx', 'fsdp'))
- key_gradient: float32 [1024, 1024], P(('ctx', 'fsdp'))
- value_gradient: float32 [1024, 1024], P(('ctx', 'fsdp'))
- query_gain_gradient: float32 [128], replicated
- key_gain_gradient: float32 [128], replicated
- output_gradient: float32 [2048, 1024], P(None, ('ctx', 'fsdp'))
- feedforward_gain_gradient: float32 [1024], replicated
- gate_gradient: float32 [1024, 3072], P(('ctx', 'fsdp'))
- up_gradient: float32 [1024, 3072], P(('ctx', 'fsdp'))
- down_gradient: float32 [3072, 1024], P(None, ('ctx', 'fsdp'))
Inputs may be any that keep to these rules, and one draw needn't show every extreme that they name: `token_positions`: each row is a permutation of the positions of one sequence. Every aligned block of 128 stored rows holds two runs of 64 consecutive rising positions, run k and run 2 * 8 - 1 - k for some k.
All inputs are finite; a program needn't handle non-finite values.
Results may differ from a plain program's by a relative error of at most 0.02.
Values may be sent and summed in bfloat16 or wider, within the bound.
A program may use at most 256 MiB of HBM per device.

v0:
```python
import functools

import jax
import jax.numpy as jnp
import numpy as np
from jax import lax
from jax.experimental import pallas as pl
from jax.experimental.pallas import tpu as pltpu
from jax.sharding import PartitionSpec as P

epsilon = 1e-06
rope_base = 1000000.0
masked_score = -1e30


def from_behind(block, axis, distance):
    devices = range(lax.axis_size(axis))
    route = [((i - distance) % len(devices), i) for i in devices]
    return lax.ppermute(block, axis, route)


def rotate(value_rows):
    half = value_rows.shape[-1] // 2
    return jnp.concatenate([-value_rows[..., half:], value_rows[..., :half]], -1)


def rotate_back(value_rows):
    half = value_rows.shape[-1] // 2
    return jnp.concatenate([value_rows[..., half:], -value_rows[..., :half]], -1)


def rope_tables(token_offsets, head_size):
    half = head_size // 2
    inverse = rope_base ** (-(jnp.arange(half).astype(jnp.float32) * 2.0) / head_size)
    angles = token_offsets.astype(jnp.float32)[:, None] * inverse[None, :]
    cosine = jnp.cos(angles)
    sine = jnp.sin(angles)
    return (jnp.concatenate([cosine, cosine], -1), jnp.concatenate([sine, sine], -1))


def norm_scale(value_rows):
    return lax.rsqrt(jnp.mean(value_rows * value_rows, -1, keepdims=True) + epsilon)


def norm_back(value_rows, scale, gain, grad):
    weighted = grad * gain
    inner = jnp.mean(weighted * value_rows, -1, keepdims=True)
    result = scale * weighted - value_rows * scale * scale * scale * inner
    gain_part = jnp.sum((grad * value_rows * scale).reshape(-1, gain.shape[0]), 0)
    return (result, gain_part)


def row_products(left, pieces):
    return tuple((jnp.dot(left, piece, preferred_element_type=jnp.float32) for piece in pieces))


def column_products(rights, pieces):
    total = jnp.einsum("tc,rc->tr", rights[0], pieces[0], preferred_element_type=jnp.float32)
    for right, piece in zip(rights[1:], pieces[1:]):
        total = total + jnp.einsum("tc,rc->tr", right, piece, preferred_element_type=jnp.float32)
    return total


def on_device(
    layer_input,
    token_positions,
    attention_gain,
    query_weight,
    key_matrix,
    value_matrix,
    query_gain,
    key_norm_gain,
    output_weight,
    feedforward_gain,
    gate_weight,
    up_weight,
    down_weight,
    out_cotangent,
):
    hidden_in = layer_input[0].astype(jnp.float32)
    count = hidden_in.shape[0]
    head_size = query_gain.shape[0]
    query_width = query_weight.shape[1]
    key_width = key_matrix.shape[1]
    inner_width = gate_weight.shape[1]
    heads = query_width // head_size
    key_heads = key_width // head_size
    group = heads // key_heads
    scale = head_size ** (-0.5)
    cycles = lax.axis_size("ctx")
    own_index = lax.axis_index("ctx")
    sequence_pos = token_positions[0]
    token_offsets = lax.dynamic_slice_in_dim(sequence_pos, own_index * count, count)
    cosine, sine = rope_tables(token_offsets, head_size)
    cosine = cosine[:, None, :]
    sine = sine[:, None, :]
    first_scale = norm_scale(hidden_in)
    first = (hidden_in * first_scale * attention_gain).astype(jnp.bfloat16)
    query_raw, key_unnormed, value_unnormed = row_products(
        first,
        (
            lax.all_gather(query_weight, "fsdp", axis=0, tiled=True),
            lax.all_gather(key_matrix, "fsdp", axis=0, tiled=True),
            lax.all_gather(value_matrix, "fsdp", axis=0, tiled=True),
        ),
    )
    query_heads = query_raw.reshape(count, heads, head_size)
    query_scale = norm_scale(query_heads)
    query_normed = query_heads * query_scale * query_gain
    query_rot = query_normed * cosine + rotate(query_normed) * sine
    query_grouped = (
        query_rot.reshape(count, key_heads, group, head_size)
        .transpose(1, 2, 0, 3)
        .astype(jnp.bfloat16)
    )
    key_heads_raw = key_unnormed.reshape(count, key_heads, head_size)
    key_scale = norm_scale(key_heads_raw)
    key_normed = key_heads_raw * key_scale * key_norm_gain
    key_low = (
        (key_normed * cosine + rotate(key_normed) * sine)
        .reshape(count, key_width)
        .astype(jnp.bfloat16)
    )
    value_low = value_unnormed.astype(jnp.bfloat16)
    rowmax = jnp.full((key_heads, group, count), masked_score, jnp.float32)
    keys_piece = lax.all_gather(key_low, "ctx", axis=0, tiled=True).reshape(
        -1, key_heads, head_size
    )
    values_piece = lax.all_gather(value_low, "ctx", axis=0, tiled=True).reshape(
        -1, key_heads, head_size
    )
    key_pos = sequence_pos
    allowed = token_offsets[:, None] >= key_pos[None, :]
    scores = (
        jnp.einsum("kgtd,skd->kgts", query_grouped, keys_piece, preferred_element_type=jnp.float32)
        * scale
    )
    scores = jnp.where(allowed, scores, masked_score)
    newmax = jnp.maximum(rowmax, jnp.max(scores, -1))
    weights = jnp.where(allowed, jnp.exp(scores - newmax[..., None]), 0.0)
    accum = jnp.einsum(
        "kgts,skd->kgtd",
        weights.astype(jnp.bfloat16),
        values_piece,
        preferred_element_type=jnp.float32,
    )
    rowsum = jnp.sum(weights, -1)
    accum, rowmax, rowsum = (accum, newmax, rowsum)
    normalized = accum / rowsum[..., None]
    logsum = rowmax + jnp.log(rowsum)
    attention_low = (
        normalized.transpose(2, 0, 1, 3).reshape(count, query_width).astype(jnp.bfloat16)
    )
    output_whole = lax.all_gather(output_weight, "fsdp", axis=0, tiled=True)
    branch_out = jnp.dot(attention_low, output_whole, preferred_element_type=jnp.float32)
    middle = hidden_in + branch_out
    second_scale = norm_scale(middle)
    second = (middle * second_scale * feedforward_gain).astype(jnp.bfloat16)
    gate, up = row_products(
        second,
        (
            lax.all_gather(gate_weight, "fsdp", axis=0, tiled=True),
            lax.all_gather(up_weight, "fsdp", axis=0, tiled=True),
        ),
    )
    sigmoid_gate = jax.nn.sigmoid(gate)
    silu_gate = gate * sigmoid_gate
    hidden_low = (silu_gate * up).astype(jnp.bfloat16)
    (down_out,) = row_products(
        hidden_low, (lax.all_gather(down_weight, "fsdp", axis=0, tiled=True),)
    )
    layer_output = (middle + down_out).astype(jnp.bfloat16)[None]
    cotangent = out_cotangent[0]
    hidden_grad = column_products(
        (cotangent,), lax.all_gather((down_weight,), "fsdp", axis=0, tiled=True)
    )
    up_low = (hidden_grad * silu_gate).astype(jnp.bfloat16)
    gate_low = (hidden_grad * up * sigmoid_gate * (1.0 + gate * (1.0 - sigmoid_gate))).astype(
        jnp.bfloat16
    )
    second_grad = column_products(
        (gate_low, up_low), lax.all_gather((gate_weight, up_weight), "fsdp", axis=0, tiled=True)
    )
    middle_part, feedforward_part = norm_back(middle, second_scale, feedforward_gain, second_grad)
    middle_grad = cotangent.astype(jnp.float32) + middle_part
    middle_low = middle_grad.astype(jnp.bfloat16)
    attention_grad = jnp.einsum(
        "tc,rc->tr", middle_low, output_whole, preferred_element_type=jnp.float32
    )
    attention_grad_low = attention_grad.astype(jnp.bfloat16)
    mixed_grad = attention_grad_low.reshape(count, key_heads, group, head_size).transpose(
        1, 2, 0, 3
    )
    delta = jnp.sum(mixed_grad.astype(jnp.float32) * normalized, -1)

    def cycle_step(index, carry):
        keys_held, values_held, key_acc, value_acc, query_acc = carry
        anchor = (own_index - index) % cycles
        key_pos = lax.dynamic_slice_in_dim(sequence_pos, anchor * count, count)
        keys_piece = keys_held.astype(jnp.bfloat16).reshape(count, key_heads, head_size)
        values_piece = values_held.astype(jnp.bfloat16).reshape(count, key_heads, head_size)
        allowed = token_offsets[:, None] >= key_pos[None, :]
        scores = (
            jnp.einsum(
                "kgtd,skd->kgts", query_grouped, keys_piece, preferred_element_type=jnp.float32
            )
            * scale
        )
        probs = jnp.where(allowed, jnp.exp(scores - logsum[..., None]), 0.0)
        value_acc = value_acc + jnp.einsum(
            "kgts,kgtd->skd",
            probs.astype(jnp.bfloat16),
            mixed_grad,
            preferred_element_type=jnp.float32,
        ).reshape(count, key_width)
        prob_grad = jnp.einsum(
            "kgtd,skd->kgts", mixed_grad, values_piece, preferred_element_type=jnp.float32
        )
        score_grad = (probs * (prob_grad - delta[..., None])).astype(jnp.bfloat16)
        query_acc = (
            query_acc
            + jnp.einsum(
                "kgts,skd->kgtd", score_grad, keys_piece, preferred_element_type=jnp.float32
            )
            * scale
        )
        key_acc = (
            key_acc
            + jnp.einsum(
                "kgts,kgtd->skd", score_grad, query_grouped, preferred_element_type=jnp.float32
            ).reshape(count, key_width)
            * scale
        )
        moved = (
            from_behind(keys_held.astype(jnp.bfloat16), "ctx", 1).astype(keys_held.dtype),
            from_behind(values_held.astype(jnp.bfloat16), "ctx", 1).astype(values_held.dtype),
            from_behind(key_acc.astype(jnp.bfloat16), "ctx", 1).astype(key_acc.dtype),
            from_behind(value_acc.astype(jnp.bfloat16), "ctx", 1).astype(value_acc.dtype),
        )
        return (moved[0], moved[1], moved[2], moved[3], query_acc)

    start_cycle = (
        key_low.astype(jnp.float32),
        value_low.astype(jnp.float32),
        jnp.zeros((count, key_width), jnp.float32),
        jnp.zeros((count, key_width), jnp.float32),
        jnp.zeros((key_heads, group, count, head_size), jnp.float32),
    )
    cycle_done = lax.fori_loop(0, cycles, cycle_step, start_cycle)
    key_acc = cycle_done[2]
    value_acc = cycle_done[3]
    query_acc = cycle_done[4]
    query_rot_grad = query_acc.transpose(2, 0, 1, 3).reshape(count, heads, head_size)
    query_normed_grad = query_rot_grad * cosine + rotate_back(query_rot_grad * sine)
    query_heads_grad, query_part = norm_back(
        query_heads, query_scale, query_gain, query_normed_grad
    )
    query_low_grad = query_heads_grad.reshape(count, query_width).astype(jnp.bfloat16)
    key_rot_grad = key_acc.reshape(count, key_heads, head_size)
    key_normed_grad = key_rot_grad * cosine + rotate_back(key_rot_grad * sine)
    key_heads_grad, key_part = norm_back(key_heads_raw, key_scale, key_norm_gain, key_normed_grad)
    key_low_grad = key_heads_grad.reshape(count, key_width).astype(jnp.bfloat16)
    value_low_grad = value_acc.astype(jnp.bfloat16)
    first_grad = column_products(
        (query_low_grad, key_low_grad, value_low_grad),
        lax.all_gather((query_weight, key_matrix, value_matrix), "fsdp", axis=0, tiled=True),
    )
    input_part, attention_part = norm_back(hidden_in, first_scale, attention_gain, first_grad)
    input_gradient = (middle_grad + input_part)[None]
    rights_first = jnp.concatenate([query_low_grad, key_low_grad, value_low_grad], 1)
    rights_second = jnp.concatenate([gate_low, up_low], 1)
    pairs = (
        (first, rights_first),
        (second, rights_second),
        (middle_low, attention_low),
        (cotangent, hidden_low),
    )
    parts = []
    for left, right in pairs:
        parts.append(jnp.einsum("tr,tc->rc", left, right, preferred_element_type=jnp.float32))
    sums = lax.psum_scatter(
        jnp.concatenate(parts, 1), ("ctx", "fsdp"), scatter_dimension=0, tiled=True
    )
    edges = [0, query_width, query_width + key_width, query_width + 2 * key_width]
    edges = edges + [edges[3] + inner_width, edges[3] + 2 * inner_width]
    edges = edges + [edges[5] + query_width, edges[5] + query_width + inner_width]
    query_gradient = sums[:, edges[0] : edges[1]]
    key_gradient = sums[:, edges[1] : edges[2]]
    value_gradient = sums[:, edges[2] : edges[3]]
    gate_gradient = sums[:, edges[3] : edges[4]]
    up_gradient = sums[:, edges[4] : edges[5]]
    output_gradient = sums[:, edges[5] : edges[6]].T
    down_gradient = sums[:, edges[6] : edges[7]].T
    attention_total, query_total, key_total, feedforward_total = lax.psum(
        (attention_part, query_part, key_part, feedforward_part), ("ctx", "fsdp")
    )
    return (
        layer_output,
        input_gradient,
        attention_total,
        query_gradient,
        key_gradient,
        value_gradient,
        query_total,
        key_total,
        output_gradient,
        feedforward_total,
        gate_gradient,
        up_gradient,
        down_gradient,
    )


MESH = pl.DeviceIdType.MESH
f32 = jnp.float32
bf16 = jnp.bfloat16


def dot(left, right):
    return jnp.dot(left, right, preferred_element_type=f32)


def dot_nt(left, right):
    return lax.dot_general(left, right, (((1,), (1,)), ((), ())), preferred_element_type=f32)


def dot_tn(left, right):
    return lax.dot_general(left, right, (((0,), (0,)), ((), ())), preferred_element_type=f32)


def hidden_block(device, third):
    def plane(i, t):
        return ((3, 1, 2), (0, 2, 1), (0, 3, 2), (3, 0, 1))[i // 4 * 2 + i % 2][t]

    own = plane(device, third)
    return own, sum(plane(i, t) == own for i in range(device) for t in range(3))


def layer_kernel(
    n, planes, block, head, group, fw,
    x_ref, dy_ref, pos_row, inverse_ref, step_cos, step_sin, ag_ref, fg_ref, qg_ref, kg_ref,
    wq, wk, wv, wo, wg, wu, wd,
    out_ref, dx_ref, gains_ref, got_a, got_b, got_c, got_out, got_qkv,
    w_qkv, w_gu, w_out, w_down, t_out,
    first, dy_all, second, first_t, dy_t, second_t,
    positions, cosine, sine,
    raw, queries, keys, values, keys_t, values_t, probs, sums, mixed_t, mixed_low,
    hidden, d_gu, d_qkv, dk_acc, dv_acc,
    stage_a, stage_b, stage_c, stage_out, stage_qkv,
    land_a, land_b, land_c, land_out, land_qkv,
    rs_sa, rs_ra, rs_sb, rs_rb, rs_kept, rs_acc,
    middle, d_middle, gain_own, gain_plane, gain_all,
    local_sem, wz_send, wz_recv, hand_send, hand_recv,
    ag_send, ag_recv, ra_send, ra_recv, rb_send, rb_recv,
    zr_send, zr_recv, aa_send, aa_recv, gp_send, gp_recv, gz_send, gz_recv,
):
    c = lax.axis_index("ctx")
    z = lax.axis_index("fsdp")
    dmid = first
    dmid_t = second
    cy, cx, ck = lax.div(c, 4), lax.rem(lax.div(c, 2), 2), lax.rem(c, 2)
    ci = lax.rem(c, 4)
    sign = 1 - 2 * ck
    qw, kw = group * head, head
    pw = 128
    thirds = fw // pw
    width = x_ref.shape[1]
    scale = head ** (-0.5)
    log2e = 1.4426950408889634
    gots = (got_a, got_b, got_c, got_out, got_qkv)
    stages = (stage_a, stage_b, stage_c, stage_out, stage_qkv)
    lands = (land_a, land_b, land_c, land_out, land_qkv)

    def partner(j):
        y = lax.rem(cy + lax.div(j, 4), 2)
        x = lax.rem(cx + lax.rem(lax.div(j, 2), 2), 2)
        k = lax.rem(ck + lax.rem(j, 2), 2)
        return y * 4 + x * 2 + k

    def chip(slot):
        return lax.rem(cy + lax.div(slot, 2), 2) * 2 + lax.rem(cx + lax.rem(slot, 2), 2)

    def rows(start, size):
        return pl.ds(pl.multiple_of(start * size, size), size)

    def remote(src, dst, send, recv, ctx, plane):
        return pltpu.make_async_remote_copy(
            src_ref=src, dst_ref=dst, send_sem=send, recv_sem=recv,
            device_id={"ctx": ctx, "fsdp": plane}, device_id_type=MESH,
        )

    in_plane, along, weight_sends = [], [], []

    def launch(started, copy, when=None):
        if when is None:
            copy().start()
        else:
            pl.when(when)(lambda: copy().start())
        started.append((copy, when))

    def drain(started):
        for copy, when in started:
            if when is None:
                copy().wait_send()
            else:
                pl.when(when)(lambda copy=copy: copy().wait_send())
        started.clear()

    def pick(values):
        return sum(jnp.where(c == i, value, 0) for i, value in enumerate(values))

    unit_plane = [pick([hidden_block(i, t)[0] for i in range(n)]) for t in range(thirds)]
    unit_block = [pick([hidden_block(i, t)[1] for i in range(n)]) for t in range(thirds)]
    plane_blocks = wd.shape[0] // pw

    own_rows = wq.shape[0]
    out_rows = wo.shape[0] // n

    def own_slices():
        mine = rows(z, own_rows)
        pairs = [
            (wq.at[:, rows(c, qw)], w_qkv.at[mine, 0:qw]),
            (wk.at[:, rows(c, kw)], w_qkv.at[mine, qw:qw + kw]),
            (wv.at[:, rows(c, kw)], w_qkv.at[mine, qw + kw:qw + 2 * kw]),
            (wo.at[rows(c, out_rows)], t_out.at[rows(z, out_rows)]),
        ]
        for t in range(thirds):
            at = 2 * pw * t
            unit = unit_plane[t] * plane_blocks + unit_block[t]
            pairs.append((wg.at[:, rows(unit, pw)], w_gu.at[mine, at:at + pw]))
            pairs.append((wu.at[:, rows(unit, pw)], w_gu.at[mine, at + pw:at + 2 * pw]))
        return pairs

    local = [pltpu.make_async_copy(src, dst, local_sem.at[i]) for i, (src, dst) in enumerate(own_slices())]
    for copy in local:
        copy.start()

    def own_down(t):
        return pltpu.make_async_copy(
            wd.at[rows(unit_block[t], pw)], w_down.at[t * pw:(t + 1) * pw], local_sem.at[4 + 2 * thirds + t])

    holds = [unit_plane[t] == z for t in range(thirds)]
    for t in range(thirds):
        pl.when(holds[t])(lambda t=t: own_down(t).start())

    for land in lands:
        @pl.when(z == 0)
        def _(land=land):
            land[0] = jnp.zeros(land.shape[1:], bf16)

        @pl.when(z == planes - 1)
        def _(land=land):
            land[planes] = jnp.zeros(land.shape[1:], bf16)

    barrier = pltpu.get_barrier_semaphore()
    for j in range(1, n):
        pl.semaphore_signal(barrier, inc=1, device_id={"ctx": partner(j), "fsdp": z}, device_id_type=MESH)
    for d in range(1, planes):
        pl.semaphore_signal(
            barrier, inc=1, device_id={"ctx": c, "fsdp": lax.rem(z + d, planes)}, device_id_type=MESH)
    x = x_ref[...].astype(f32)
    x_scale = lax.rsqrt(jnp.mean(x * x, -1, keepdims=True) + epsilon)
    first[rows(c, block)] = (x * x_scale * ag_ref[...]).astype(bf16)
    dy_all[rows(c, block)] = dy_ref[...]
    for copy in local[:3]:
        copy.wait()
    pl.semaphore_wait(barrier, n + planes - 2)

    def inside(t):
        return jnp.logical_and(t >= 0, t < planes)

    weights = [
        (lambda o: w_qkv.at[rows(o, own_rows)], None),
        (lambda o: t_out.at[rows(o, out_rows)], 0),
    ]
    for t in range(thirds):
        weights.append((lambda o, t=t: w_gu.at[rows(o, own_rows), 2 * pw * t:2 * pw * (t + 1)], None))
        weights.append((lambda o, t=t: w_down.at[t * pw:(t + 1) * pw], None))

    def weight_copy(w, slot, origin, target):
        part = weights[w][0](origin)
        return remote(part, part, wz_send.at[w, slot], wz_recv.at[w, origin], c, target)

    def from_plane(w, origin):
        return origin == unit_plane[(w - 3) // 2] if w >= 3 and w % 2 else None

    def both(one, other):
        return one if other is None else jnp.logical_and(one, other)

    def hand_split(origin, valid):
        mine = 2 * origin + cy == c
        return jnp.logical_and(valid, jnp.logical_not(mine)), jnp.logical_and(valid, mine)

    def weight_start(w):
        for side in range(2):
            d = sign * (1 - 2 * side)
            launch(
                weight_sends, lambda side=side, d=d: weight_copy(w, side, z, z + d),
                both(inside(z + d), from_plane(w, z)))
        if weights[w][1] is not None:
            hand_over(w, z, 0, *hand_split(z, True))

    def hand_target(h):
        return lambda i: w_out.at[rows(i, out_rows)]

    def hand_copy(w, origin, slot):
        h = weights[w][1]
        return remote(
            weights[w][0](origin), hand_target(h)(ci), hand_send.at[h, slot], hand_recv.at[h, ci], 2 * origin + cy, z)

    def hand_over(w, origin, slot, away, here):
        launch(in_plane, lambda: hand_copy(w, origin, slot), away)

        @pl.when(here)
        def _():
            hand_target(weights[w][1])(ci)[...] = weights[w][0](origin)[...]

    def hand_arrive(w):
        h = weights[w][1]
        for i in range(4):
            @pl.when(4 * ck + i != c)
            def _(i=i):
                part = hand_target(h)(i)
                remote(part, part, hand_send.at[h, 0], hand_recv.at[h, i], c, z).wait_recv()

    hops = {}
    for w in range(len(weights)):
        for d in range(1, planes):
            for side, way in enumerate((1, -1)):
                origin = z - way * d
                valid = both(inside(origin), from_plane(w, origin))
                passed = jnp.logical_and(valid, inside(z + way))
                split = None if weights[w][1] is None else hand_split(origin, valid)
                hops[w, d, side] = origin, z + way, valid, passed, split

    def weight_hop(w, d):
        for side in range(2):
            origin, following, valid, passed, split = hops[w, d, side]
            pl.when(valid)(lambda: weight_copy(w, 0, origin, z).wait_recv())
            if d < planes - 1:
                launch(
                    weight_sends,
                    lambda side=side, origin=origin, following=following: weight_copy(
                        w, 2 * d + side, origin, following),
                    passed)
            if split is not None:
                hand_over(w, origin, 2 * d - 1 + side, *split)

    def gather_copy(buf, g, j, send, origin, target):
        part = buf.at[rows(origin, block)]
        return remote(part, part, ag_send.at[g, send], ag_recv.at[g, j], target, z)

    def gather_start(buf, g):
        for j in (1, 2 + 2 * ck, 4 - 2 * ck):
            launch(in_plane, lambda j=j: gather_copy(buf, g, j, j, c, partner(j)))

    def gather_half(buf, g, j):
        half = block // 2
        part = buf.at[pl.ds(pl.multiple_of(partner(j) * block + (half if j == 2 else 0), half), half)]
        at = 0 if j == 2 else 6
        return remote(part, part, ag_send.at[g, at], ag_recv.at[g, at], partner(6 - j), z)

    def gather_diagonal(buf, g):
        half = block // 2
        for at in (6, 0):
            part = buf.at[pl.ds(pl.multiple_of(partner(6) * block + (0 if at == 6 else half), half), half)]
            remote(part, part, ag_send.at[g, at], ag_recv.at[g, at], c, z).wait_recv()

    def gather_forward(buf, g, j):
        return gather_copy(buf, g, j + 1, j + 1, partner(j), partner(1))

    def gather_take(buf, g, j):
        if j == 6:
            gather_diagonal(buf, g)
        else:
            gather_copy(buf, g, j, j, partner(j), c).wait_recv()
            gather_half(buf, g, j).start()
        gather_forward(buf, g, j).start()

    def gather_sent(buf, g):
        for j in (2, 4, 6):
            in_plane.append((lambda j=j: gather_forward(buf, g, j), None))
            if j < 6:
                in_plane.append((lambda j=j: gather_half(buf, g, j), None))

    def gather_finish(buf, g):
        for j in (2, 4, 6):
            gather_take(buf, g, j)
        gather_sent(buf, g)
        for j in (1, 3, 5, 7):
            gather_copy(buf, g, j, j, partner(j), c).wait_recv()

    def gather_step(buf, g, slot):
        @pl.when(slot == 1)
        def _():
            gather_take(buf, g, 2)
            gather_take(buf, g, 4)

        pl.when(slot == 3)(lambda: gather_take(buf, g, 6))
        gather_copy(buf, g, 2 * slot + 1, 0, partner(2 * slot + 1), c).wait_recv()

    def sum_pair_copy(s, slot):
        return remote(rs_sa.at[s % 2, slot], rs_ra.at[s % 2, slot], ra_send.at[s, slot], ra_recv.at[s, slot], partner(1), z)

    def sum_chip_copy(s, slot):
        return remote(
            rs_sb.at[s % 2, slot], rs_rb.at[s % 2, slot], rb_send.at[s, slot], rb_recv.at[s, slot], partner(2 * slot), z)

    def sum_half_copy(s, slot):
        half = block // 2
        at = pl.ds(pl.multiple_of((slot - 1) * half, half), half)
        return remote(
            rs_sb.at[s % 2, 3, at], rs_rb.at[s % 2, 3, at], rb_send.at[s, 6 - 3 * slot], rb_recv.at[s, 6 - 3 * slot],
            partner(6 - 2 * slot), z)

    def sum_slot(p):
        return jnp.where(p == 0, 3, jnp.where(p == 1, 2 - ck, jnp.where(p == 2, 1 + ck, 0)))

    def sum_start(s, left, partial, prepare=None, ready=None, during=()):
        if prepare is not None:
            prepare(chip(sum_slot(0)))
        if ready is not None:
            ready()

        def body(p, carry):
            slot = sum_slot(p)
            at = [rows(partner(2 * slot + 1), block), rows(partner(2 * slot), block)]
            both = partial(jnp.concatenate([left[i] for i in at], 0))
            rs_sa[s % 2, slot] = both[:block].astype(bf16)
            sum_pair_copy(s, slot).start()
            rs_kept[lax.rem(p, 2)] = both[block:]

            @pl.when(p > 0)
            def _():
                before = sum_slot(p - 1)
                sum_pair_copy(s, before).wait_recv()
                rs_sb[s % 2, before] = (
                    rs_kept[lax.rem(p + 1, 2)] + rs_ra[s % 2, before].astype(f32)).astype(bf16)

            @pl.when(p == 1)
            def _():
                sum_half_copy(s, 1).start()
                sum_half_copy(s, 2).start()

            @pl.when(p > 1)
            def _():
                before = sum_slot(p - 1)
                half = block // 2
                at = pl.ds(pl.multiple_of((before - 1) * half, half), half)
                sum_half_copy(s, before).wait_recv()
                rs_sb[s % 2, before, at] = (
                    rs_sb[s % 2, before, at].astype(f32) + rs_rb[s % 2, 3, at].astype(f32)).astype(bf16)
                sum_chip_copy(s, before).start()

            if prepare is not None:
                @pl.when(p < 3)
                def _():
                    prepare(chip(sum_slot(p + 1)))

            for k, poll in enumerate(during):
                pl.when(p == k)(poll)
            return carry

        lax.fori_loop(0, 4, body, 0)
        for slot in range(4):
            in_plane.append((lambda slot=slot: sum_pair_copy(s, slot), None))
        for slot in (1, 2):
            in_plane.append((lambda slot=slot: sum_half_copy(s, slot), None))
            in_plane.append((lambda slot=slot: sum_chip_copy(s, slot), None))
        sum_pair_copy(s, 0).wait_recv()
        rs_acc[s % 2] = rs_kept[1] + rs_ra[s % 2, 0].astype(f32)

    def sum_finish(s):
        total = rs_acc[s % 2]
        for slot in (1, 2):
            sum_chip_copy(s, slot).wait_recv()
            total = total + rs_rb[s % 2, slot].astype(f32)
        return total

    per = block // planes

    def weight_grad(m, parts):
        def body(i, carry):
            at = 0
            for left, right in parts:
                value = right()
                grad = dot(left[rows(i, 4 * block)], value)
                for k in range(4):
                    for t in range(planes):
                        start = k * block + t * per
                        stages[m][t, 4 * i + k, :, at:at + value.shape[1]] = grad[start:start + per].astype(bf16)
                at += value.shape[1]
            return carry

        lax.fori_loop(0, n // 4, body, 0)
        at_edge = jnp.logical_or(z == 0, z == planes - 1)
        for k in range(planes - 1):
            t = jnp.where(z == 0, planes - 1 - k, k)
            launch(along, lambda t=t: grad_copy(m, t), at_edge)

    def grad_copy(m, t):
        way = jnp.where(z < t, 1, -1)
        last = z + way == t
        slot = jnp.where(jnp.logical_and(last, way < 0), planes, t)
        return remote(
            stages[m].at[t], lands[m].at[slot], zr_send.at[m, t], zr_recv.at[m, slot], c, z + way)

    def grad_arrive(m, slot):
        part = lands[m].at[slot]
        remote(part, part, zr_send.at[m, 0], zr_recv.at[m, slot], c, z).wait_recv()

    def grad_pass(m, t, valid):
        @pl.when(valid)
        def _():
            grad_arrive(m, t)

            def body(i, carry):
                stages[m][t, i] = (stages[m][t, i].astype(f32) + lands[m][t, i].astype(f32)).astype(bf16)
                return carry

            lax.fori_loop(0, n, body, 0)

        launch(along, lambda: grad_copy(m, t), valid)

    is_low, is_high = z == 1, z == planes - 2

    def grad_near_far(m):
        grad_pass(m, 3, is_low)
        grad_pass(m, 0, is_high)

    def grad_near_inner(m):
        grad_pass(m, 2, is_low)
        grad_pass(m, 1, is_high)

    def grad_near(m):
        grad_near_far(m)
        grad_near_inner(m)

    def grad_far(m):
        grad_pass(m, 3, is_high)
        grad_pass(m, 0, is_low)

    def owner_copy(m, j):
        return remote(lands[m].at[z, partner(j)], gots[m].at[c], aa_send.at[m, j], aa_recv.at[m, j], partner(j), z)

    def hand_out(m):
        pl.when(z > 0)(lambda: grad_arrive(m, z))
        pl.when(z < planes - 1)(lambda: grad_arrive(m, planes))

        def body(i, carry):
            total = stages[m][z, i].astype(f32) + lands[m][z, i].astype(f32) + lands[m][planes, i].astype(f32)
            lands[m][z, i] = total.astype(bf16)
            return carry

        lax.fori_loop(0, n, body, 0)
        for j in (2 + 2 * ck, 3 + 2 * ck, 4 - 2 * ck, 5 - 2 * ck, 6, 7, 1):
            launch(in_plane, lambda j=j: owner_copy(m, j))
        gots[m][c] = lands[m][z, c]

    def hand_receive(m):
        for j in range(1, n):
            owner_copy(m, j).wait_recv()

    weight_start(0)
    gather_start(first, 0)
    for copy in local[3:]:
        copy.wait()
    for t in range(thirds):
        pl.when(holds[t])(lambda t=t: own_down(t).wait())

    spread = jnp.broadcast_to(pos_row[...].astype(f32), (head, pos_row.shape[1]))
    positions[...] = spread.T
    side = jnp.where(lax.broadcasted_iota(jnp.int32, (1, head), 1) < head // 2, -1.0, 1.0)

    def table(i, carry):
        run = step_cos.shape[0]
        at = rows(i, run)
        start = positions[pl.ds(pl.multiple_of(i * run, run), 1)] * inverse_ref[...]
        start_cos, start_sin = jnp.cos(start), jnp.sin(start)
        cosine[at] = start_cos * step_cos[...] - start_sin * step_sin[...]
        sine[at] = (start_sin * step_cos[...] + start_cos * step_sin[...]) * side
        return carry

    def turn_over(src, dst):
        def body(i, carry):
            at = rows(i, block)
            dst[:, at] = src[at].T
            return carry

        lax.fori_loop(0, n, body, 0)

    lax.fori_loop(0, 2 * n, table, 0)
    weight_hop(0, 1)
    gather_finish(first, 0)
    weight_hop(0, 2)
    weight_start(1)
    gather_start(dy_all, 1)
    turn_over(first, first_t)
    weight_hop(0, 3)
    weight_start(2)
    weight_start(3)

    def turn(value, at):
        return value * cosine[at] + pltpu.roll(value, head // 2, 1) * sine[at]

    def turn_back(grad, at):
        return grad * cosine[at] - pltpu.roll(grad, head // 2, 1) * sine[at]

    def project(i, carry):
        at = rows(i, 2 * block)
        result = dot(first[at], w_qkv[...])
        raw[at] = result[:, :qw + kw]
        low_values = result[:, qw + kw:].astype(bf16)
        values[at] = low_values
        values_t[:, at] = low_values.T
        for h in range(group + 1):
            part = result[:, h * head:(h + 1) * head]
            inv = lax.rsqrt(jnp.mean(part * part, -1, keepdims=True) + epsilon)
            gain = qg_ref[...] if h < group else kg_ref[...]
            turned = turn(part * inv * gain, at)
            if h < group:
                queries[at, h * head:(h + 1) * head] = (turned * (scale * log2e)).astype(bf16)
            else:
                low_keys = turned.astype(bf16)
                keys[at] = low_keys
                keys_t[:, at] = low_keys.T
        return carry

    lax.fori_loop(0, n // 4, project, 0)
    weight_hop(1, 1)
    lax.fori_loop(n // 4, n // 2, project, 0)
    weight_hop(1, 2)
    gather_finish(dy_all, 1)

    def stack(ref, at):
        return jnp.concatenate([ref[at, h * head:(h + 1) * head] for h in range(group)], 0)

    def attend(place):
        at = rows(place, 2 * block)
        scores = dot_nt(keys[...], stack(queries, at))
        allowed = positions[...] <= pos_row[:, rows(2 * place, block)].astype(f32)
        later = positions[...] <= pos_row[:, rows(2 * place + 1, block)].astype(f32)
        weight = jnp.concatenate(
            [jnp.exp2(jnp.where(later if k % 2 else allowed, scores[:, k * block:(k + 1) * block], masked_score))
             for k in range(2 * group)], 1)
        inv = 1.0 / jnp.sum(weight, 0, keepdims=True)
        low_weight = weight.astype(bf16)
        probs[place] = low_weight
        sums[place] = inv
        result = dot(values_t[...], low_weight) * inv
        mixed_t[place] = result
        for h in range(group):
            mixed_low[at, h * head:(h + 1) * head] = result[:, 2 * h * block:2 * (h + 1) * block].T.astype(bf16)

    def output_ready():
        weight_hop(1, 3)
        weight_start(4)
        weight_start(5)
        hand_arrive(1)
        drain(in_plane)

    def hop_third(t, d):
        weight_hop(2 + 2 * t, d)
        weight_hop(3 + 2 * t, d)

    sum_start(
        0, mixed_low, lambda left: dot(left, w_out[...]), attend, output_ready,
        (lambda: hop_third(0, 1), lambda: hop_third(0, 2), lambda: hop_third(1, 1)))
    weight_start(6)
    weight_start(7)
    hop_third(0, 3)
    turn_over(dy_all, dy_t)
    hop_third(1, 2)
    mid = x_ref[...].astype(f32) + sum_finish(0)
    middle[...] = mid
    mid_scale = lax.rsqrt(jnp.mean(mid * mid, -1, keepdims=True) + epsilon)
    second[rows(c, block)] = (mid * mid_scale * fg_ref[...]).astype(bf16)
    gather_start(second, 2)
    hop_third(2, 1)

    def feed(t, at):
        units, pair = slice(t * pw, (t + 1) * pw), 2 * pw * t
        both = dot(second[at], w_gu[:, pair:pair + 2 * pw])
        back = dot_nt(dy_all[at], w_down[units])
        gate, up = both[:, :pw], both[:, pw:]
        sig = 1.0 / (1.0 + jnp.exp(-gate))
        silu = gate * sig
        hidden[at, units] = (silu * up).astype(bf16)
        d_gu[at, pair:pair + pw] = (back * up * sig * (1.0 + gate * (1.0 - sig))).astype(bf16)
        d_gu[at, pair + pw:pair + 2 * pw] = (back * silu).astype(bf16)

    def feed_arriving(slot, carry):
        gather_step(second, 2, slot)
        at = rows(chip(slot), 2 * block)
        feed(0, at)
        second_t[:, at] = second[at].T
        pl.when(slot == 2)(lambda: hop_third(2, 2))
        return carry

    def third_grad(t):
        weight_grad(t, [
            (second_t, lambda: d_gu[:, 2 * pw * t:2 * pw * (t + 1)]),
            (dy_t, lambda: hidden[:, t * pw:(t + 1) * pw]),
        ])

    def feed_third(t):
        def body(i, carry):
            feed(t, rows(i, 2 * block))
            return carry

        lax.fori_loop(0, n // 2, body, 0)

    lax.fori_loop(0, n // 2, feed_arriving, 0)
    gather_sent(second, 2)
    hop_third(1, 3)
    third_grad(0)
    feed_third(1)
    hop_third(2, 3)
    sum_start(
        1, d_gu, lambda left: dot_nt(left, w_gu[...]),
        lambda place: feed(thirds - 1, rows(place, 2 * block)))
    third_grad(1)
    third_grad(2)
    d_second = sum_finish(1)

    def norm_back(value, gain, grad):
        inv = lax.rsqrt(jnp.mean(value * value, -1, keepdims=True) + epsilon)
        weighted = grad * gain
        inner = jnp.mean(weighted * value, -1, keepdims=True)
        result = inv * weighted - value * (inv * inv * inv * inner)
        return result, jnp.sum(grad * value * inv, 0, keepdims=True)

    gain_own[...] = jnp.zeros_like(gain_own)
    part, gain_own[1:2, :] = norm_back(middle[...], fg_ref[...], d_second)
    d_mid = dy_ref[...].astype(f32) + part
    d_middle[...] = d_mid
    drain(in_plane)
    dmid[rows(c, block)] = d_mid.astype(bf16)
    gather_start(dmid, 3)
    drain(weight_sends)
    grad_near(0)

    dk_acc[...] = jnp.zeros_like(dk_acc)
    dv_acc[...] = jnp.zeros_like(dv_acc)

    def attend_back(slot, q_sum):
        gather_step(dmid, 3, slot)
        place = chip(slot)
        at = rows(place, 2 * block)
        d_mix = dot_nt(w_out[...], dmid[at])
        dmid_t[:, at] = dmid[at].T
        d_mix_t = jnp.concatenate([d_mix[h * head:(h + 1) * head] for h in range(group)], 1)
        d_mix_t = (d_mix_t.astype(bf16).astype(f32) * sums[place]).astype(bf16)
        delta = jnp.sum(d_mix_t.astype(f32) * mixed_t[place], 0, keepdims=True)
        weight = probs[place]
        d_prob = dot(values[...], d_mix_t)
        d_score = (weight.astype(f32) * (d_prob - delta)).astype(bf16)
        d_query = dot(keys_t[...], d_score) * scale
        for h in range(group):
            grad = turn_back(d_query[:, 2 * h * block:2 * (h + 1) * block].T, at)
            part, gain_part = norm_back(raw[at, h * head:(h + 1) * head], qg_ref[...], grad)
            d_qkv[at, h * head:(h + 1) * head] = part.astype(bf16)
            q_sum = q_sum + gain_part
        pl.when(slot == 2)(lambda: grad_near(1))
        dv_acc[...] += dot(weight, d_mix_t.T)
        dk_acc[...] += dot(d_score, stack(queries, at))
        return q_sum

    zero = jnp.zeros((1, head), f32)
    gain_own[2:3, 0:head] = lax.fori_loop(0, n // 2, attend_back, zero)
    gather_sent(dmid, 3)
    weight_grad(3, [(dmid_t, lambda: mixed_low[...])])
    grad_far(0)
    drain(in_plane)
    sum_start(2, hidden, lambda left: dot(left, w_down[...]))

    def project_back(i, k_sum):
        at = rows(i, 2 * block)
        grad = turn_back(dk_acc[at] * (1.0 / log2e), at)
        part, gain_part = norm_back(raw[at, qw:qw + kw], kg_ref[...], grad)
        d_qkv[at, qw:qw + kw] = part.astype(bf16)
        d_qkv[at, qw + kw:] = dv_acc[at].astype(bf16)
        return k_sum + gain_part

    gain_own[3:4, 0:head] = lax.fori_loop(0, n // 2, project_back, zero)

    weight_grad(4, [(first_t, lambda: d_qkv[...])])
    grad_far(1)
    grad_near(2)
    hand_out(0)
    sum_start(3, d_qkv, lambda left: dot_nt(left, w_qkv[...]))
    grad_far(2)
    grad_near(3)
    grad_near_far(4)
    out_ref[...] = (middle[...] + sum_finish(2)).astype(bf16)
    hand_out(1)
    grad_far(3)
    grad_near_inner(4)
    grad_far(4)
    x_part, gain_own[0:1, :] = norm_back(x_ref[...].astype(f32), ag_ref[...], sum_finish(3))
    dx_ref[...] = d_middle[...] + x_part

    def gain_plane_copy(j):
        return remote(gain_own, gain_plane.at[c], gp_send.at[j], gp_recv.at[j], partner(j), z)

    def gain_copy(d):
        return remote(gain_all.at[z], gain_all.at[z], gz_send.at[d], gz_recv.at[d], c, lax.rem(z + d, planes))

    for j in range(1, n):
        launch(in_plane, lambda j=j: gain_plane_copy(j))
    gain_plane[c] = gain_own[...]
    hand_out(2)
    for j in range(1, n):
        gain_plane_copy(j).wait_recv()
    total = gain_plane[0]
    for i in range(1, n):
        total = total + gain_plane[i]
    gain_all[z] = total
    for d in range(1, planes):
        launch(along, lambda d=d: gain_copy(d))
    hand_out(3)
    for d in range(1, planes):
        origin = gain_all.at[lax.rem(z + planes - d, planes)]
        remote(origin, origin, gz_send.at[d], gz_recv.at[d], c, z).wait_recv()
    total = gain_all[0]
    for i in range(1, planes):
        total = total + gain_all[i]
    gains_ref[...] = total

    for m in range(4):
        hand_receive(m)
    drain(in_plane)
    hand_out(4)
    drain(along)
    hand_receive(4)
    drain(in_plane)


def finish_kernel(
    n, head, out_in, dx_in, gains_in, got_a, got_b, got_c, got_out, got_qkv,
    out_ref, dx_ref, ag_ref, q_ref, k_ref, v_ref, qg_ref, kg_ref, o_ref, fg_ref, g_ref, u_ref, d_ref,
):
    out_ref[...] = out_in[...]
    dx_ref[...] = dx_in[...]
    ag_ref[...] = gains_in[0:1, :]
    fg_ref[...] = gains_in[1:2, :]
    qg_ref[...] = gains_in[2:3, 0:head]
    kg_ref[...] = gains_in[3:4, 0:head]
    qw, kw = q_ref.shape[1] // n, k_ref.shape[1] // n
    pw = got_a.shape[2] // 3
    thirds = (got_a, got_b, got_c)
    for i in range(n):
        q_ref[:, i * qw:(i + 1) * qw] = got_qkv[i, :, 0:qw].astype(f32)
        k_ref[:, i * kw:(i + 1) * kw] = got_qkv[i, :, qw:qw + kw].astype(f32)
        v_ref[:, i * kw:(i + 1) * kw] = got_qkv[i, :, qw + kw:].astype(f32)
        o_ref[:, i * qw:(i + 1) * qw] = got_out[i].astype(f32)
        for t, got in enumerate(thirds):
            plane, unit = hidden_block(i, t)
            at = plane * (g_ref.shape[1] // 4) + unit * pw
            g_ref[:, at:at + pw] = got[i, :, 0:pw].astype(f32)
            u_ref[:, at:at + pw] = got[i, :, pw:2 * pw].astype(f32)
            d_ref[:, at:at + pw] = got[i, :, 2 * pw:].astype(f32)


def plane_device(
    layer_input,
    token_positions,
    attention_gain,
    query_weight,
    key_matrix,
    value_matrix,
    query_gain,
    key_norm_gain,
    output_weight,
    feedforward_gain,
    gate_weight,
    up_weight,
    down_weight,
    out_cotangent,
):
    n = lax.axis_size("ctx")
    planes = lax.axis_size("fsdp")
    block, width = layer_input.shape[1:]
    length = token_positions.shape[1]
    head = query_gain.shape[0]
    qw = query_weight.shape[1] // n
    kw = key_matrix.shape[1] // n
    fw = gate_weight.shape[1] // n
    group = qw // head
    per = block // planes
    half = head // 2
    inverse = np.power(rope_base, -np.arange(half) * 2.0 / head).astype(np.float32)
    inverse = np.concatenate([inverse, inverse])[None]
    steps = np.arange(block // 2)[:, None] * inverse.astype(np.float64)
    step_cos, step_sin = (jnp.asarray(f(steps).astype(np.float32)) for f in (np.cos, np.sin))
    inverse = jnp.asarray(inverse)
    vmem = pl.BlockSpec(memory_space=pltpu.VMEM)
    hbm = pl.BlockSpec(memory_space=pl.ANY)
    dma = pltpu.SemaphoreType.DMA
    sizes = (fw, fw, fw, qw, qw + 2 * kw)
    low = lambda *shape: pltpu.VMEM(shape, bf16)
    wide = lambda *shape: pltpu.VMEM(shape, f32)
    scratch = [
        low(width, qw + 2 * kw), low(width, 2 * fw), low(qw, width), low(fw, width),
        low(planes * (output_weight.shape[0] // n), width),
        low(length, width), low(length, width), low(length, width),
        low(width, length), low(width, length), low(width, length),
        wide(length, head), wide(length, head), wide(length, head),
        wide(length, qw + kw), low(length, qw), low(length, kw), low(length, kw),
        low(kw, length), low(kw, length), low(n // 2, length, 2 * group * block), wide(n // 2, 1, 2 * group * block),
        wide(n // 2, head, 2 * group * block), low(length, qw),
        low(length, fw), low(length, 2 * fw), low(length, qw + 2 * kw),
        wide(length, kw), wide(length, kw),
    ]
    scratch += [low(planes, n, per, size) for size in sizes]
    scratch += [low(planes + 1, n, per, size) for size in sizes]
    scratch += [low(2, 4, block, width) for _ in range(4)] + [wide(2, block, width), wide(2, block, width)]
    scratch += [
        wide(block, width), wide(block, width), wide(8, width), wide(n, 8, width), wide(planes, 8, width),
        dma((13,)), dma((8, 6)), dma((8, planes)), dma((1, 7)), dma((1, 4)),
        dma((4, n)), dma((4, n)), dma((4, 4)), dma((4, 4)), dma((4, 4)), dma((4, 4)),
        dma((5, planes)), dma((5, planes + 1)), dma((5, n)), dma((5, n)), dma((n,)), dma((n,)),
        dma((planes,)), dma((planes,)),
    ]
    shapes = [
        jax.ShapeDtypeStruct((block, width), bf16),
        jax.ShapeDtypeStruct((block, width), f32),
        jax.ShapeDtypeStruct((8, width), f32),
    ] + [jax.ShapeDtypeStruct((n, per, size), bf16) for size in sizes]
    results = pl.pallas_call(
        functools.partial(layer_kernel, n, planes, block, head, group, fw),
        out_shape=shapes,
        in_specs=[vmem] * 10 + [hbm] * 7,
        out_specs=[vmem] * len(shapes),
        scratch_shapes=scratch,
        compiler_params=pltpu.CompilerParams(
            collective_id=0, has_side_effects=True, vmem_limit_bytes=60 * 1024 * 1024),
    )(
        layer_input[0], out_cotangent[0], token_positions, inverse, step_cos, step_sin,
        attention_gain[None], feedforward_gain[None], query_gain[None], key_norm_gain[None],
        query_weight, key_matrix, value_matrix, output_weight, gate_weight, up_weight, down_weight,
    )
    plain = lambda rows, columns, kind=f32: jax.ShapeDtypeStruct((rows, columns), kind)
    finals = [
        plain(block, width, bf16), plain(block, width), plain(1, width),
        plain(per, n * qw), plain(per, n * kw), plain(per, n * kw), plain(1, head), plain(1, head),
        plain(per, n * qw), plain(1, width), plain(per, n * fw), plain(per, n * fw), plain(per, n * fw),
    ]
    done = pl.pallas_call(
        functools.partial(finish_kernel, n, head),
        out_shape=finals,
        in_specs=[vmem] * len(shapes),
        out_specs=[vmem] * len(finals),
    )(*results)
    out, dx, ag, q, k, v, qg, kg, o, fg, g, u, d = done
    return out[None], dx[None], ag[0], q, k, v, qg[0], kg[0], o.T, fg[0], g, u, d.T


def solution(mesh):
    in_specs = (
        P("fsdp", "ctx", None),
        P("fsdp", None),
        P(),
        P("fsdp", None),
        P("fsdp", None),
        P("fsdp", None),
        P(),
        P(),
        P("fsdp", None),
        P(),
        P("fsdp", None),
        P("fsdp", None),
        P("fsdp", None),
        P("fsdp", "ctx", None),
    )
    out_specs = (
        P("fsdp", "ctx", None),
        P("fsdp", "ctx", None),
        P(),
        P(("ctx", "fsdp"), None),
        P(("ctx", "fsdp"), None),
        P(("ctx", "fsdp"), None),
        P(),
        P(),
        P(None, ("ctx", "fsdp")),
        P(),
        P(("ctx", "fsdp"), None),
        P(("ctx", "fsdp"), None),
        P(None, ("ctx", "fsdp")),
    )

    def run(*arguments):
        n, planes = mesh.shape["ctx"], mesh.shape["fsdp"]
        key_heads = arguments[4].shape[1] // arguments[6].shape[0]
        whole_heads = n == 8 and planes == 4 and key_heads == n
        return jax.shard_map(
            plane_device if whole_heads else on_device,
            mesh=mesh, in_specs=in_specs, out_specs=out_specs, check_vma=False,
        )(*arguments)

    return run
```

profile of v0, /device:TPU:0, one launch (start us, length us, event | category | flops | bytes accessed | tf_op | source)
XLA Modules:
  0.0 172.3 jit_solution(12055738725745501083)
XLA Ops:
  0.7 168.6 %shard_map.264 = (bf16[128,1024]{1,0:T(8,128)(2,1)}, f32[128,1024]{1,0:T(8,128)}, f32[8,1024]{1,0:T(8,128)}, bf16[8,32,384]{2,1,0:T(8,128)(2,1)}, bf16[8,32,384]...) custom-call(bf16[128,1024]{1,0:T(8,128)(2,1)} %bitcast.14, ...), custom_call_target="tpu_custom_call" | custom-call | tf_op jit(solution)/shard_map/pallas_call | solution.py:1130
  169.3 3.1 %shard_map.265 = (bf16[128,1024]{1,0:T(8,128)(2,1)}, f32[128,1024]{1,0:T(8,128)}, f32[1,1024]{1,0:T(1,128)}, f32[32,2048]{1,0:T(8,128)}, f32[32,1024]{1,0:T(8,12...) custom-call(bf16[128,1024]{1,0:T(8,128)(2,1)} %get-tuple-element.34., ...), custom_call_target="tpu_custom_call" | custom-call | tf_op jit(solution)/shard_map/pallas_call | solution.py:1149
where the time goes:
time: 173 us; the launch traced here: 172 us
  Pallas kernels  172 us (99%)
    pallas_call x1, Pallas kernels, plane_device(): pl.pallas_call(functools.partial(layer_kernel, n, planes, block, head, gr...  169 us

commit v1 on v0

--- a/solution.py
+++ b/solution.py
@@ -340,14 +340,14 @@
     n, planes, block, head, group, fw,
     x_ref, dy_ref, pos_row, inverse_ref, step_cos, step_sin, ag_ref, fg_ref, qg_ref, kg_ref,
     wq, wk, wv, wo, wg, wu, wd,
-    out_ref, dx_ref, gains_ref, got_a, got_b, got_c, got_out, got_qkv,
+    out_ref, dx_ref, gains_ref, got_a, got_b, got_c, got_out, got_q, got_kv,
     w_qkv, w_gu, w_out, w_down, t_out,
     first, dy_all, second, first_t, dy_t, second_t,
     positions, cosine, sine,
     raw, queries, keys, values, keys_t, values_t, probs, sums, mixed_t, mixed_low,
     hidden, d_gu, d_qkv, dk_acc, dv_acc,
-    stage_a, stage_b, stage_c, stage_out, stage_qkv,
-    land_a, land_b, land_c, land_out, land_qkv,
+    stage_a, stage_b, stage_c, stage_out, stage_q, stage_kv,
+    land_a, land_b, land_c, land_out, land_q, land_kv,
     rs_sa, rs_ra, rs_sb, rs_rb, rs_kept, rs_acc,
     middle, d_middle, gain_own, gain_plane, gain_all,
     local_sem, wz_send, wz_recv, hand_send, hand_recv,
@@ -367,9 +367,9 @@
     width = x_ref.shape[1]
     scale = head ** (-0.5)
     log2e = 1.4426950408889634
-    gots = (got_a, got_b, got_c, got_out, got_qkv)
-    stages = (stage_a, stage_b, stage_c, stage_out, stage_qkv)
-    lands = (land_a, land_b, land_c, land_out, land_qkv)
+    gots = (got_a, got_b, got_c, got_out, got_q, got_kv)
+    stages = (stage_a, stage_b, stage_c, stage_out, stage_q, stage_kv)
+    lands = (land_a, land_b, land_c, land_out, land_q, land_kv)
 
     def partner(j):
         y = lax.rem(cy + lax.div(j, 4), 2)
@@ -679,6 +679,9 @@
 
     per = block // planes
 
+    at_edge = jnp.logical_or(z == 0, z == planes - 1)
+    edge_targets = [jnp.where(z == 0, planes - 1 - k, k) for k in range(planes - 1)]
+
     def weight_grad(m, parts):
         def body(i, carry):
             at = 0
@@ -693,9 +696,7 @@
             return carry
 
         lax.fori_loop(0, n // 4, body, 0)
-        at_edge = jnp.logical_or(z == 0, z == planes - 1)
-        for k in range(planes - 1):
-            t = jnp.where(z == 0, planes - 1 - k, k)
+        for t in edge_targets:
             launch(along, lambda t=t: grad_copy(m, t), at_edge)
 
     def grad_copy(m, t):
@@ -937,6 +938,7 @@
     drain(in_plane)
     dmid[rows(c, block)] = d_mid.astype(bf16)
     gather_start(dmid, 3)
+    sum_start(2, hidden, lambda left: dot(left, w_down[...]))
     drain(weight_sends)
     grad_near(0)
 
@@ -949,6 +951,7 @@
         at = rows(place, 2 * block)
         d_mix = dot_nt(w_out[...], dmid[at])
         dmid_t[:, at] = dmid[at].T
+        pl.when(slot == 3)(lambda: weight_grad(3, [(dmid_t, lambda: mixed_low[...])]))
         d_mix_t = jnp.concatenate([d_mix[h * head:(h + 1) * head] for h in range(group)], 1)
         d_mix_t = (d_mix_t.astype(bf16).astype(f32) * sums[place]).astype(bf16)
         delta = jnp.sum(d_mix_t.astype(f32) * mixed_t[place], 0, keepdims=True)
@@ -969,10 +972,8 @@
     zero = jnp.zeros((1, head), f32)
     gain_own[2:3, 0:head] = lax.fori_loop(0, n // 2, attend_back, zero)
     gather_sent(dmid, 3)
-    weight_grad(3, [(dmid_t, lambda: mixed_low[...])])
+    weight_grad(4, [(first_t, lambda: d_qkv[:, :qw])])
     grad_far(0)
-    drain(in_plane)
-    sum_start(2, hidden, lambda left: dot(left, w_down[...]))
 
     def project_back(i, k_sum):
         at = rows(i, 2 * block)
@@ -984,19 +985,23 @@
 
     gain_own[3:4, 0:head] = lax.fori_loop(0, n // 2, project_back, zero)
 
-    weight_grad(4, [(first_t, lambda: d_qkv[...])])
+    weight_grad(5, [(first_t, lambda: d_qkv[:, qw:])])
     grad_far(1)
     grad_near(2)
     hand_out(0)
+    drain(in_plane)
     sum_start(3, d_qkv, lambda left: dot_nt(left, w_qkv[...]))
     grad_far(2)
     grad_near(3)
-    grad_near_far(4)
-    out_ref[...] = (middle[...] + sum_finish(2)).astype(bf16)
     hand_out(1)
     grad_far(3)
-    grad_near_inner(4)
+    grad_near(4)
+    out_ref[...] = (middle[...] + sum_finish(2)).astype(bf16)
     grad_far(4)
+    grad_near_far(5)
+    hand_out(2)
+    grad_near_inner(5)
+    grad_far(5)
     x_part, gain_own[0:1, :] = norm_back(x_ref[...].astype(f32), ag_ref[...], sum_finish(3))
     dx_ref[...] = d_middle[...] + x_part
 
@@ -1009,7 +1014,7 @@
     for j in range(1, n):
         launch(in_plane, lambda j=j: gain_plane_copy(j))
     gain_plane[c] = gain_own[...]
-    hand_out(2)
+    hand_out(3)
     for j in range(1, n):
         gain_plane_copy(j).wait_recv()
     total = gain_plane[0]
@@ -1018,7 +1023,7 @@
     gain_all[z] = total
     for d in range(1, planes):
         launch(along, lambda d=d: gain_copy(d))
-    hand_out(3)
+    hand_out(4)
     for d in range(1, planes):
         origin = gain_all.at[lax.rem(z + planes - d, planes)]
         remote(origin, origin, gz_send.at[d], gz_recv.at[d], c, z).wait_recv()
@@ -1029,15 +1034,15 @@
 
     for m in range(4):
         hand_receive(m)
-    drain(in_plane)
-    hand_out(4)
+    hand_out(5)
     drain(along)
     hand_receive(4)
+    hand_receive(5)
     drain(in_plane)
 
 
 def finish_kernel(
-    n, head, out_in, dx_in, gains_in, got_a, got_b, got_c, got_out, got_qkv,
+    n, head, out_in, dx_in, gains_in, got_a, got_b, got_c, got_out, got_q, got_kv,
     out_ref, dx_ref, ag_ref, q_ref, k_ref, v_ref, qg_ref, kg_ref, o_ref, fg_ref, g_ref, u_ref, d_ref,
 ):
     out_ref[...] = out_in[...]
@@ -1050,9 +1055,9 @@
     pw = got_a.shape[2] // 3
     thirds = (got_a, got_b, got_c)
     for i in range(n):
-        q_ref[:, i * qw:(i + 1) * qw] = got_qkv[i, :, 0:qw].astype(f32)
-        k_ref[:, i * kw:(i + 1) * kw] = got_qkv[i, :, qw:qw + kw].astype(f32)
-        v_ref[:, i * kw:(i + 1) * kw] = got_qkv[i, :, qw + kw:].astype(f32)
+        q_ref[:, i * qw:(i + 1) * qw] = got_q[i].astype(f32)
+        k_ref[:, i * kw:(i + 1) * kw] = got_kv[i, :, 0:kw].astype(f32)
+        v_ref[:, i * kw:(i + 1) * kw] = got_kv[i, :, kw:].astype(f32)
         o_ref[:, i * qw:(i + 1) * qw] = got_out[i].astype(f32)
         for t, got in enumerate(thirds):
             plane, unit = hidden_block(i, t)
@@ -1097,7 +1102,7 @@
     vmem = pl.BlockSpec(memory_space=pltpu.VMEM)
     hbm = pl.BlockSpec(memory_space=pl.ANY)
     dma = pltpu.SemaphoreType.DMA
-    sizes = (fw, fw, fw, qw, qw + 2 * kw)
+    sizes = (fw, fw, fw, qw, qw, 2 * kw)
     low = lambda *shape: pltpu.VMEM(shape, bf16)
     wide = lambda *shape: pltpu.VMEM(shape, f32)
     scratch = [
@@ -1119,7 +1124,7 @@
         wide(block, width), wide(block, width), wide(8, width), wide(n, 8, width), wide(planes, 8, width),
         dma((13,)), dma((8, 6)), dma((8, planes)), dma((1, 7)), dma((1, 4)),
         dma((4, n)), dma((4, n)), dma((4, 4)), dma((4, 4)), dma((4, 4)), dma((4, 4)),
-        dma((5, planes)), dma((5, planes + 1)), dma((5, n)), dma((5, n)), dma((n,)), dma((n,)),
+        dma((6, planes)), dma((6, planes + 1)), dma((6, n)), dma((6, n)), dma((n,)), dma((n,)),
         dma((planes,)), dma((planes,)),
     ]
     shapes = [

time: 173 us -> 174 us (level)
  no operation moved by 1% of the time
where the time goes in v1:
time: 174 us; the launch traced here: 173 us
  Pallas kernels  173 us (99%)
    pallas_call x1, Pallas kernels, plane_device(): pl.pallas_call(functools.partial(layer_kernel, n, planes, block, head, gr...  170 us

profile of v1, /device:TPU:0, one launch (start us, length us, event | category | flops | bytes accessed | tf_op | source)
XLA Modules:
  0.0 173.3 jit_solution(13032518510222141827)
XLA Ops:
  0.7 169.7 %shard_map.264 = (bf16[128,1024]{1,0:T(8,128)(2,1)}, f32[128,1024]{1,0:T(8,128)}, f32[8,1024]{1,0:T(8,128)}, bf16[8,32,384]{2,1,0:T(8,128)(2,1)}, bf16[8,32,384]...) custom-call(bf16[128,1024]{1,0:T(8,128)(2,1)} %bitcast.14, ...), custom_call_target="tpu_custom_call" | custom-call | tf_op jit(solution)/shard_map/pallas_call | solution.py:1135
  170.3 3.0 %shard_map.265 = (bf16[128,1024]{1,0:T(8,128)(2,1)}, f32[128,1024]{1,0:T(8,128)}, f32[1,1024]{1,0:T(1,128)}, f32[32,2048]{1,0:T(8,128)}, f32[32,1024]{1,0:T(8,12...) custom-call(bf16[128,1024]{1,0:T(8,128)(2,1)} %get-tuple-element.35., ...), custom_call_target="tpu_custom_call" | custom-call | tf_op jit(solution)/shard_map/pallas_call | solution.py:1154

commit v2 on v1

--- a/solution.py
+++ b/solution.py
@@ -340,14 +340,15 @@
     n, planes, block, head, group, fw,
     x_ref, dy_ref, pos_row, inverse_ref, step_cos, step_sin, ag_ref, fg_ref, qg_ref, kg_ref,
     wq, wk, wv, wo, wg, wu, wd,
-    out_ref, dx_ref, gains_ref, got_a, got_b, got_c, got_out, got_q, got_kv,
+    out_ref, dx_ref, gains_ref, got_ab, got_co, got_qkv,
     w_qkv, w_gu, w_out, w_down, t_out,
     first, dy_all, second, first_t, dy_t, second_t,
     positions, cosine, sine,
-    raw, queries, keys, values, keys_t, values_t, probs, sums, mixed_t, mixed_low,
+    raw, queries, keys, values, keys_t, values_t, probs, sums, mixed_t, mixed_low, mixed_low_t,
     hidden, d_gu, d_qkv, dk_acc, dv_acc,
     stage_a, stage_b, stage_c, stage_out, stage_q, stage_kv,
     land_a, land_b, land_c, land_out, land_q, land_kv,
+    own_ab, own_co, own_qkv,
     rs_sa, rs_ra, rs_sb, rs_rb, rs_kept, rs_acc,
     middle, d_middle, gain_own, gain_plane, gain_all,
     local_sem, wz_send, wz_recv, hand_send, hand_recv,
@@ -357,7 +358,6 @@
     c = lax.axis_index("ctx")
     z = lax.axis_index("fsdp")
     dmid = first
-    dmid_t = second
     cy, cx, ck = lax.div(c, 4), lax.rem(lax.div(c, 2), 2), lax.rem(c, 2)
     ci = lax.rem(c, 4)
     sign = 1 - 2 * ck
@@ -367,7 +367,8 @@
     width = x_ref.shape[1]
     scale = head ** (-0.5)
     log2e = 1.4426950408889634
-    gots = (got_a, got_b, got_c, got_out, got_q, got_kv)
+    gots = (got_ab, got_co, got_qkv)
+    owns = (own_ab, own_co, own_qkv)
     stages = (stage_a, stage_b, stage_c, stage_out, stage_q, stage_kv)
     lands = (land_a, land_b, land_c, land_out, land_q, land_kv)
 
@@ -604,13 +605,13 @@
 
     def sum_chip_copy(s, slot):
         return remote(
-            rs_sb.at[s % 2, slot], rs_rb.at[s % 2, slot], rb_send.at[s, slot], rb_recv.at[s, slot], partner(2 * slot), z)
+            rs_sb.at[s % 2, slot - 1], rs_rb.at[s % 2, slot - 1], rb_send.at[s, slot], rb_recv.at[s, slot], partner(2 * slot), z)
 
     def sum_half_copy(s, slot):
         half = block // 2
         at = pl.ds(pl.multiple_of((slot - 1) * half, half), half)
         return remote(
-            rs_sb.at[s % 2, 3, at], rs_rb.at[s % 2, 3, at], rb_send.at[s, 6 - 3 * slot], rb_recv.at[s, 6 - 3 * slot],
+            rs_sb.at[s % 2, 2, at], rs_rb.at[s % 2, 2, at], rb_send.at[s, 6 - 3 * slot], rb_recv.at[s, 6 - 3 * slot],
             partner(6 - 2 * slot), z)
 
     def sum_slot(p):
@@ -634,7 +635,7 @@
             def _():
                 before = sum_slot(p - 1)
                 sum_pair_copy(s, before).wait_recv()
-                rs_sb[s % 2, before] = (
+                rs_sb[s % 2, before - 1] = (
                     rs_kept[lax.rem(p + 1, 2)] + rs_ra[s % 2, before].astype(f32)).astype(bf16)
 
             @pl.when(p == 1)
@@ -648,8 +649,8 @@
                 half = block // 2
                 at = pl.ds(pl.multiple_of((before - 1) * half, half), half)
                 sum_half_copy(s, before).wait_recv()
-                rs_sb[s % 2, before, at] = (
-                    rs_sb[s % 2, before, at].astype(f32) + rs_rb[s % 2, 3, at].astype(f32)).astype(bf16)
+                rs_sb[s % 2, before - 1, at] = (
+                    rs_sb[s % 2, before - 1, at].astype(f32) + rs_rb[s % 2, 2, at].astype(f32)).astype(bf16)
                 sum_chip_copy(s, before).start()
 
             if prepare is not None:
@@ -674,7 +675,7 @@
         total = rs_acc[s % 2]
         for slot in (1, 2):
             sum_chip_copy(s, slot).wait_recv()
-            total = total + rs_rb[s % 2, slot].astype(f32)
+            total = total + rs_rb[s % 2, slot - 1].astype(f32)
         return total
 
     per = block // planes
@@ -696,6 +697,9 @@
             return carry
 
         lax.fori_loop(0, n // 4, body, 0)
+        grad_send(m)
+
+    def grad_send(m):
         for t in edge_targets:
             launch(along, lambda t=t: grad_copy(m, t), at_edge)
 
@@ -714,12 +718,7 @@
         @pl.when(valid)
         def _():
             grad_arrive(m, t)
-
-            def body(i, carry):
-                stages[m][t, i] = (stages[m][t, i].astype(f32) + lands[m][t, i].astype(f32)).astype(bf16)
-                return carry
-
-            lax.fori_loop(0, n, body, 0)
+            stages[m][t] = stages[m][t] + lands[m][t]
 
         launch(along, lambda: grad_copy(m, t), valid)
 
@@ -741,26 +740,27 @@
         grad_pass(m, 3, is_high)
         grad_pass(m, 0, is_low)
 
-    def owner_copy(m, j):
-        return remote(lands[m].at[z, partner(j)], gots[m].at[c], aa_send.at[m, j], aa_recv.at[m, j], partner(j), z)
-
-    def hand_out(m):
+    def owner_copy(g, j):
+        return remote(owns[g].at[partner(j)], gots[g].at[c], aa_send.at[g, j], aa_recv.at[g, j], partner(j), z)
+
+    def own_sum(m):
         pl.when(z > 0)(lambda: grad_arrive(m, z))
         pl.when(z < planes - 1)(lambda: grad_arrive(m, planes))
-
-        def body(i, carry):
-            total = stages[m][z, i].astype(f32) + lands[m][z, i].astype(f32) + lands[m][planes, i].astype(f32)
-            lands[m][z, i] = total.astype(bf16)
-            return carry
-
-        lax.fori_loop(0, n, body, 0)
+        total = stages[m][z].astype(f32) + lands[m][z].astype(f32) + lands[m][planes].astype(f32)
+        first_size = stages[m // 2 * 2].shape[3]
+        if m % 2:
+            owns[m // 2][:, :, first_size:] = total.astype(bf16)
+        else:
+            owns[m // 2][:, :, :first_size] = total.astype(bf16)
+
+    def hand_out(g):
         for j in (2 + 2 * ck, 3 + 2 * ck, 4 - 2 * ck, 5 - 2 * ck, 6, 7, 1):
-            launch(in_plane, lambda j=j: owner_copy(m, j))
-        gots[m][c] = lands[m][z, c]
-
-    def hand_receive(m):
+            launch(in_plane, lambda j=j: owner_copy(g, j))
+        gots[g][c] = owns[g][c]
+
+    def hand_receive(g):
         for j in range(1, n):
-            owner_copy(m, j).wait_recv()
+            owner_copy(g, j).wait_recv()
 
     weight_start(0)
     gather_start(first, 0)
@@ -851,7 +851,9 @@
         result = dot(values_t[...], low_weight) * inv
         mixed_t[place] = result
         for h in range(group):
-            mixed_low[at, h * head:(h + 1) * head] = result[:, 2 * h * block:2 * (h + 1) * block].T.astype(bf16)
+            low_result = result[:, 2 * h * block:2 * (h + 1) * block].astype(bf16)
+            mixed_low_t[h * head:(h + 1) * head, at] = low_result
+            mixed_low[at, h * head:(h + 1) * head] = low_result.T
 
     def output_ready():
         weight_hop(1, 3)
@@ -945,13 +947,24 @@
     dk_acc[...] = jnp.zeros_like(dk_acc)
     dv_acc[...] = jnp.zeros_like(dv_acc)
 
+    def output_grad():
+        def body(i, carry):
+            grad = dot(mixed_low_t[...], dmid[:, rows(i, 2 * block)]).astype(bf16).T
+            for k in range(2):
+                for t in range(planes):
+                    start = k * block + t * per
+                    stage_out[t, 2 * i + k] = grad[start:start + per]
+            return carry
+
+        lax.fori_loop(0, n // 2, body, 0)
+        grad_send(3)
+
     def attend_back(slot, q_sum):
         gather_step(dmid, 3, slot)
         place = chip(slot)
         at = rows(place, 2 * block)
         d_mix = dot_nt(w_out[...], dmid[at])
-        dmid_t[:, at] = dmid[at].T
-        pl.when(slot == 3)(lambda: weight_grad(3, [(dmid_t, lambda: mixed_low[...])]))
+        pl.when(slot == 3)(output_grad)
         d_mix_t = jnp.concatenate([d_mix[h * head:(h + 1) * head] for h in range(group)], 1)
         d_mix_t = (d_mix_t.astype(bf16).astype(f32) * sums[place]).astype(bf16)
         delta = jnp.sum(d_mix_t.astype(f32) * mixed_t[place], 0, keepdims=True)
@@ -988,18 +1001,19 @@
     weight_grad(5, [(first_t, lambda: d_qkv[:, qw:])])
     grad_far(1)
     grad_near(2)
-    hand_out(0)
+    own_sum(0)
     drain(in_plane)
     sum_start(3, d_qkv, lambda left: dot_nt(left, w_qkv[...]))
     grad_far(2)
     grad_near(3)
-    hand_out(1)
+    own_sum(1)
+    hand_out(0)
     grad_far(3)
     grad_near(4)
     out_ref[...] = (middle[...] + sum_finish(2)).astype(bf16)
     grad_far(4)
     grad_near_far(5)
-    hand_out(2)
+    own_sum(2)
     grad_near_inner(5)
     grad_far(5)
     x_part, gain_own[0:1, :] = norm_back(x_ref[...].astype(f32), ag_ref[...], sum_finish(3))
@@ -1014,7 +1028,8 @@
     for j in range(1, n):
         launch(in_plane, lambda j=j: gain_plane_copy(j))
     gain_plane[c] = gain_own[...]
-    hand_out(3)
+    own_sum(3)
+    hand_out(1)
     for j in range(1, n):
         gain_plane_copy(j).wait_recv()
     total = gain_plane[0]
@@ -1023,7 +1038,7 @@
     gain_all[z] = total
     for d in range(1, planes):
         launch(along, lambda d=d: gain_copy(d))
-    hand_out(4)
+    own_sum(4)
     for d in range(1, planes):
         origin = gain_all.at[lax.rem(z + planes - d, planes)]
         remote(origin, origin, gz_send.at[d], gz_recv.at[d], c, z).wait_recv()
@@ -1032,17 +1047,17 @@
         total = total + gain_all[i]
     gains_ref[...] = total
 
-    for m in range(4):
-        hand_receive(m)
-    hand_out(5)
+    hand_receive(0)
+    own_sum(5)
+    hand_out(2)
     drain(along)
-    hand_receive(4)
-    hand_receive(5)
+    hand_receive(1)
+    hand_receive(2)
     drain(in_plane)
 
 
 def finish_kernel(
-    n, head, out_in, dx_in, gains_in, got_a, got_b, got_c, got_out, got_q, got_kv,
+    n, head, out_in, dx_in, gains_in, got_ab, got_co, got_qkv,
     out_ref, dx_ref, ag_ref, q_ref, k_ref, v_ref, qg_ref, kg_ref, o_ref, fg_ref, g_ref, u_ref, d_ref,
 ):
     out_ref[...] = out_in[...]
@@ -1052,19 +1067,20 @@
     qg_ref[...] = gains_in[2:3, 0:head]
     kg_ref[...] = gains_in[3:4, 0:head]
     qw, kw = q_ref.shape[1] // n, k_ref.shape[1] // n
-    pw = got_a.shape[2] // 3
-    thirds = (got_a, got_b, got_c)
+    fw = g_ref.shape[1] // n
+    pw = fw // 3
+    thirds = ((got_ab, 0), (got_ab, fw), (got_co, 0))
     for i in range(n):
-        q_ref[:, i * qw:(i + 1) * qw] = got_q[i].astype(f32)
-        k_ref[:, i * kw:(i + 1) * kw] = got_kv[i, :, 0:kw].astype(f32)
-        v_ref[:, i * kw:(i + 1) * kw] = got_kv[i, :, kw:].astype(f32)
-        o_ref[:, i * qw:(i + 1) * qw] = got_out[i].astype(f32)
-        for t, got in enumerate(thirds):
+        q_ref[:, i * qw:(i + 1) * qw] = got_qkv[i, :, 0:qw].astype(f32)
+        k_ref[:, i * kw:(i + 1) * kw] = got_qkv[i, :, qw:qw + kw].astype(f32)
+        v_ref[:, i * kw:(i + 1) * kw] = got_qkv[i, :, qw + kw:].astype(f32)
+        o_ref[:, i * qw:(i + 1) * qw] = got_co[i, :, fw:].astype(f32)
+        for t, (got, start) in enumerate(thirds):
             plane, unit = hidden_block(i, t)
             at = plane * (g_ref.shape[1] // 4) + unit * pw
-            g_ref[:, at:at + pw] = got[i, :, 0:pw].astype(f32)
-            u_ref[:, at:at + pw] = got[i, :, pw:2 * pw].astype(f32)
-            d_ref[:, at:at + pw] = got[i, :, 2 * pw:].astype(f32)
+            g_ref[:, at:at + pw] = got[i, :, start:start + pw].astype(f32)
+            u_ref[:, at:at + pw] = got[i, :, start + pw:start + 2 * pw].astype(f32)
+            d_ref[:, at:at + pw] = got[i, :, start + 2 * pw:start + 3 * pw].astype(f32)
 
 
 def plane_device(
@@ -1113,25 +1129,26 @@
         wide(length, head), wide(length, head), wide(length, head),
         wide(length, qw + kw), low(length, qw), low(length, kw), low(length, kw),
         low(kw, length), low(kw, length), low(n // 2, length, 2 * group * block), wide(n // 2, 1, 2 * group * block),
-        wide(n // 2, head, 2 * group * block), low(length, qw),
+        wide(n // 2, head, 2 * group * block), low(length, qw), low(qw, length),
         low(length, fw), low(length, 2 * fw), low(length, qw + 2 * kw),
         wide(length, kw), wide(length, kw),
     ]
     scratch += [low(planes, n, per, size) for size in sizes]
     scratch += [low(planes + 1, n, per, size) for size in sizes]
-    scratch += [low(2, 4, block, width) for _ in range(4)] + [wide(2, block, width), wide(2, block, width)]
+    scratch += [low(n, per, sizes[m] + sizes[m + 1]) for m in (0, 2, 4)]
+    scratch += [low(2, 4, block, width)] * 2 + [low(2, 3, block, width)] * 2 + [wide(2, block, width), wide(2, block, width)]
     scratch += [
         wide(block, width), wide(block, width), wide(8, width), wide(n, 8, width), wide(planes, 8, width),
         dma((13,)), dma((8, 6)), dma((8, planes)), dma((1, 7)), dma((1, 4)),
         dma((4, n)), dma((4, n)), dma((4, 4)), dma((4, 4)), dma((4, 4)), dma((4, 4)),
-        dma((6, planes)), dma((6, planes + 1)), dma((6, n)), dma((6, n)), dma((n,)), dma((n,)),
+        dma((6, planes)), dma((6, planes + 1)), dma((3, n)), dma((3, n)), dma((n,)), dma((n,)),
         dma((planes,)), dma((planes,)),
     ]
     shapes = [
         jax.ShapeDtypeStruct((block, width), bf16),
         jax.ShapeDtypeStruct((block, width), f32),
         jax.ShapeDtypeStruct((8, width), f32),
-    ] + [jax.ShapeDtypeStruct((n, per, size), bf16) for size in sizes]
+    ] + [jax.ShapeDtypeStruct((n, per, sizes[m] + sizes[m + 1]), bf16) for m in (0, 2, 4)]
     results = pl.pallas_call(
         functools.partial(layer_kernel, n, planes, block, head, group, fw),
         out_shape=shapes,

time: 174 us -> 172 us (0.989)
  Pallas kernels: 173 us -> 171 us
where the time goes in v2:
time: 172 us
  Pallas kernels  171 us (99%)
    pallas_call x1, Pallas kernels, plane_device(): pl.pallas_call(functools.partial(layer_kernel, n, planes, block, head, gr...  168 us

profile of v2, /device:TPU:0, one launch (start us, length us, event | category | flops | bytes accessed | tf_op | source)
XLA Modules:
  0.0 172.1 jit_solution(14204375216345148855)
XLA Ops:
  0.7 168.5 %shard_map.264 = (bf16[128,1024]{1,0:T(8,128)(2,1)}, f32[128,1024]{1,0:T(8,128)}, f32[8,1024]{1,0:T(8,128)}, bf16[8,32,768]{2,1,0:T(8,128)(2,1)}, bf16[8,32,640]...) custom-call(bf16[128,1024]{1,0:T(8,128)(2,1)} %bitcast.14, bf16[128,1024]{1,0:T(8,128)(2,1)} %bitcast.15, s32[1,1024]{1,0:T(1,128)} %pos_row.1, ...), custom_call_target="tpu_custom_call" | custom-call | tf_op jit(solution)/shard_map/pallas_call | solution.py:1152
  169.1 3.0 %shard_map.265 = (bf16[128,1024]{1,0:T(8,128)(2,1)}, f32[128,1024]{1,0:T(8,128)}, f32[1,1024]{1,0:T(1,128)}, f32[32,2048]{1,0:T(8,128)}, f32[32,1024]{1,0:T(8,12...) custom-call(bf16[128,1024]{1,0:T(8,128)(2,1)} %get-tuple-element.32., ...), custom_call_target="tpu_custom_call" | custom-call | tf_op jit(solution)/shard_map/pallas_call | solution.py:1171

commit v3 on v2

--- a/solution.py
+++ b/solution.py
@@ -426,10 +426,9 @@
             (wo.at[rows(c, out_rows)], t_out.at[rows(z, out_rows)]),
         ]
         for t in range(thirds):
-            at = 2 * pw * t
             unit = unit_plane[t] * plane_blocks + unit_block[t]
-            pairs.append((wg.at[:, rows(unit, pw)], w_gu.at[mine, at:at + pw]))
-            pairs.append((wu.at[:, rows(unit, pw)], w_gu.at[mine, at + pw:at + 2 * pw]))
+            pairs.append((wg.at[:, rows(unit, pw)], w_gu.at[t, mine, 0:pw]))
+            pairs.append((wu.at[:, rows(unit, pw)], w_gu.at[t, mine, pw:2 * pw]))
         return pairs
 
     local = [pltpu.make_async_copy(src, dst, local_sem.at[i]) for i, (src, dst) in enumerate(own_slices())]
@@ -475,7 +474,7 @@
         (lambda o: t_out.at[rows(o, out_rows)], 0),
     ]
     for t in range(thirds):
-        weights.append((lambda o, t=t: w_gu.at[rows(o, own_rows), 2 * pw * t:2 * pw * (t + 1)], None))
+        weights.append((lambda o, t=t: w_gu.at[t, rows(o, own_rows)], None))
         weights.append((lambda o, t=t: w_down.at[t * pw:(t + 1) * pw], None))
 
     def weight_copy(w, slot, origin, target):
@@ -883,7 +882,7 @@
 
     def feed(t, at):
         units, pair = slice(t * pw, (t + 1) * pw), 2 * pw * t
-        both = dot(second[at], w_gu[:, pair:pair + 2 * pw])
+        both = dot(second[at], w_gu[t])
         back = dot_nt(dy_all[at], w_down[units])
         gate, up = both[:, :pw], both[:, pw:]
         sig = 1.0 / (1.0 + jnp.exp(-gate))
@@ -920,7 +919,7 @@
     feed_third(1)
     hop_third(2, 3)
     sum_start(
-        1, d_gu, lambda left: dot_nt(left, w_gu[...]),
+        1, d_gu, lambda left: sum(dot_nt(left[:, 2 * pw * t:2 * pw * (t + 1)], w_gu[t]) for t in range(thirds)),
         lambda place: feed(thirds - 1, rows(place, 2 * block)))
     third_grad(1)
     third_grad(2)
@@ -1122,7 +1121,7 @@
     low = lambda *shape: pltpu.VMEM(shape, bf16)
     wide = lambda *shape: pltpu.VMEM(shape, f32)
     scratch = [
-        low(width, qw + 2 * kw), low(width, 2 * fw), low(qw, width), low(fw, width),
+        low(width, qw + 2 * kw), low(3, width, 2 * fw // 3), low(qw, width), low(fw, width),
         low(planes * (output_weight.shape[0] // n), width),
         low(length, width), low(length, width), low(length, width),
         low(width, length), low(width, length), low(width, length),

time: 172 us -> 173 us (level)
  no operation moved by 1% of the time
where the time goes in v3:
time: 173 us; the launch traced here: 172 us
  Pallas kernels  172 us (99%)
    pallas_call x1, Pallas kernels, plane_device(): pl.pallas_call(functools.partial(layer_kernel, n, planes, block, head, gr...  169 us

profile of v3, /device:TPU:0, one launch (start us, length us, event | category | flops | bytes accessed | tf_op | source)
XLA Modules:
  0.0 172.4 jit_solution(17141198140982556562)
XLA Ops:
  0.7 168.8 %shard_map.264 = (bf16[128,1024]{1,0:T(8,128)(2,1)}, f32[128,1024]{1,0:T(8,128)}, f32[8,1024]{1,0:T(8,128)}, bf16[8,32,768]{2,1,0:T(8,128)(2,1)}, bf16[8,32,640]...) custom-call(bf16[128,1024]{1,0:T(8,128)(2,1)} %bitcast.14, bf16[128,1024]{1,0:T(8,128)(2,1)} %bitcast.15, s32[1,1024]{1,0:T(1,128)} %pos_row.1, ...), custom_call_target="tpu_custom_call" | custom-call | tf_op jit(solution)/shard_map/pallas_call | solution.py:1151
  169.4 3.0 %shard_map.265 = (bf16[128,1024]{1,0:T(8,128)(2,1)}, f32[128,1024]{1,0:T(8,128)}, f32[1,1024]{1,0:T(1,128)}, f32[32,2048]{1,0:T(8,128)}, f32[32,1024]{1,0:T(8,12...) custom-call(bf16[128,1024]{1,0:T(8,128)(2,1)} %get-tuple-element.32., ...), custom_call_target="tpu_custom_call" | custom-call | tf_op jit(solution)/shard_map/pallas_call | solution.py:1170
